TPU v7x, 512 devices: a whole 4x8x8 slice. The times are simulated.
512 devices in a mesh: layer: 4 (over x), seq: 16 (over y, core), tile: 8 (over z).
Axes of the slice: x: 4, y: 8, z: 8, core: 2. Of those that a mesh axis runs over, the one named last changes fastest.
Arguments:
- activations: bfloat16 [16, 3072, 4096], P('layer', 'seq', 'tile'), parts along dimension 0, may hold values from -6 to 6
- out_grads: bfloat16 [16, 3072, 14336], P('layer', 'seq', 'tile'), parts along dimension 0, may hold values from -6 to 6
- proj_in: bfloat16 [16384, 128], P(('layer', 'tile')), parts along dimension 0, may hold values from -0.09375 to 0.09375
- proj_out: bfloat16 [57344, 256], P(('layer', 'tile')), parts along dimension 0, may hold values from -0.046875 to 0.046875
- seq_lengths: int32 [4], replicated, may hold values from 1 to 3072, 7680 in all
- tile_map: int32 [128, 2], replicated, may hold values from 0 to 127, as said below
- prior_cov: float32 [512, 256, 256], P(('layer', 'seq', 'tile')), parts along dimension 0, may hold values from -6 to 6
Outputs:
- covariance: float32 [512, 256, 256], P(('layer', 'seq', 'tile')), parts along dimension 0
There are 4 independent parts, one for each index of `layer`. A program takes and returns all parts, laid end to end along the dimension named above; an argument that names none is the same for every part. Nothing has to cross between parts.
Inputs may be any that keep to these rules, and one draw needn't show every extreme that they name: `tile_map`: each row holds two feature block numbers, the first not above the second; rows may repeat.
All inputs are finite; a program needn't handle non-finite values.
Results may differ from a plain program's by a relative error of at most 0.0003.
Values sent between devices are 32-bit elements; how exact they have to be, the bound alone decides.
No kernel may reach another device: no remote copies, remote signals or barrier semaphores. Data moves between devices by JAX's collectives and lax.ppermute only.
A program may use at most 192 MiB of HBM per device.

v0:
```python
import jax
import jax.numpy as jnp
from jax import lax
from jax.sharding import PartitionSpec as P


def project_tokens(act_rows, grad_rows, proj_in, proj_out):
    left_side = jnp.einsum("slc,ck->lsk", act_rows, proj_in, preferred_element_type=jnp.float32)
    right_side = jnp.einsum("slc,ck->lsk", grad_rows, proj_out, preferred_element_type=jnp.float32)
    return jnp.concatenate([left_side, right_side], axis=2)


def body(activations, out_grads, proj_in, proj_out, seq_lengths, tile_map, prior_cov):
    tiles_here = prior_cov.shape[0]
    block_size = prior_cov.shape[1]
    seq_count = activations.shape[0]
    tok_len = activations.shape[1]
    width_in = proj_in.shape[1]
    width_out = proj_out.shape[1]
    tile_count = lax.axis_size("tile")
    tok_rows = tok_len // tile_count
    whole_term = project_tokens(activations, out_grads, proj_in, proj_out)
    totals = lax.psum(whole_term, "tile")
    summed = lax.dynamic_slice_in_dim(totals, lax.axis_index("tile") * tok_rows, tok_rows, 0)
    positions = (
        lax.axis_index("seq") * tok_len
        + lax.axis_index("tile") * tok_rows
        + jnp.arange(tok_rows, dtype=jnp.int32)
    )
    token_mask = (positions[:, None] < seq_lengths[None, :]).astype(jnp.float32)
    token_weight = token_mask * lax.rsqrt(seq_lengths.astype(jnp.float32))[None, :]
    left_part = summed[:, :, :width_in]
    right_part = summed[:, :, width_in:] * token_weight[:, :, None]
    partial_value = jnp.einsum(
        "lsj,lsi->sji", right_part, left_part, precision=lax.Precision.HIGHEST
    )
    partial_value = partial_value.reshape(seq_count, width_out * width_in)
    offsets = jnp.arange(block_size, dtype=jnp.int32)
    features = lax.psum_scatter(partial_value, ("seq", "tile"), scatter_dimension=1, tiled=True)
    owner_index = lax.axis_index(("seq", "tile"))
    own_pairs = lax.dynamic_slice_in_dim(tile_map, owner_index * tiles_here, tiles_here, 0)
    shard_piece = lax.all_gather(features, ("seq", "tile"), axis=1, tiled=True)
    piece_width = shard_piece.shape[1]
    columns = own_pairs[:, :, None] * block_size + offsets
    inside = (columns >= 0) & (columns < piece_width)
    picked = jnp.take(shard_piece, jnp.clip(columns, 0, piece_width - 1), axis=1)
    picked = jnp.where(inside[None], picked, 0.0)
    chosen = jnp.transpose(picked, (1, 2, 0, 3))
    product = jnp.einsum(
        "kse,ksf->kef", chosen[:, 0], chosen[:, 1], precision=lax.Precision.HIGHEST
    )
    return prior_cov + product


def solution(mesh):
    return jax.shard_map(
        body,
        mesh=mesh,
        in_specs=(
            P("layer", "seq", "tile"),
            P("layer", "seq", "tile"),
            P(("layer", "tile"), None),
            P(("layer", "tile"), None),
            P(),
            P(),
            P(("layer", "seq", "tile"), None, None),
        ),
        out_specs=P(("layer", "seq", "tile"), None, None),
        check_vma=False,
    )
```

profile of v0, /device:TPU:25, one launch (start us, length us, event | category | flops | bytes accessed | tf_op | source)
XLA Modules:
  0.0 484.0 jit_solution(7159621079205856472)
XLA Ops:
  6.5 0.0 copy-start
  6.5 0.0 copy-start.1
  6.5 0.0 all-reduce.2.cloned.1.call-start
  6.5 1.8 copy-done
  8.3 0.0 copy-start.3
  8.3 2.1 convolution_bitcast_fusion
  10.4 0.0 copy-done.1
  10.4 0.0 copy-done.3
  10.4 0.4 convolution_bitcast_fusion.1
  10.8 1.1 pad_maximum_fusion
  11.9 0.0 copy-start.5
  11.9 0.0 all-reduce.2.cloned.1.call-update
  12.0 0.0 reduce-scatter.2.cloned.1.call-start
  12.0 0.6 copy-done.5
  12.6 0.1 compare_select_fusion.2
  12.7 82.7 %all-reduce.2.cloned.1.call-done = f32[192,4,384]{2,0,1:T(8,128)} async-done(((f32[192,4,384]{2,0,1:T(8,128)}), f32[192,4,384]{2,0,1:T(8,128)}) %all-reduce.2.cloned.1.call-update) | async-done | bytes 1179664 | tf_op jit(solution)/shard_map/psum | solution.py:23
  95.4 2.0 fusion.3
  97.4 8.7 %copy.10 = f32[4,256,128]{0,2,1:T(8,128)} copy(f32[4,256,128]{2,1,0:T(8,128)S(1)} %fusion.3) | data formatting | bytes 1048576 | tf_op jit(solution)/shard_map/reshape | solution.py:37
  106.1 0.0 copy-start.4
  106.1 0.0 reduce-scatter.2.cloned.1.call-update
  106.1 0.6 copy-done.4
  106.7 0.2 multiply_reduce_fusion
  106.9 0.1 fusion.6
  107.0 0.1 compare_and_fusion.1
  107.1 0.0 copy-start.2
  107.1 220.6 %reduce-scatter.2.cloned.1.call-done = f32[4,256]{0,1:T(8,128)} async-done(((f32[4,32768]{0,1:T(8,128)}), f32[4,256]{0,1:T(8,128)}) %reduce-scatter.2.cloned.1.call-update) | async-done | bytes 4112 | tf_op jit(solution)/shard_map/reduce_scatter | solution.py:39
  327.7 141.3 %all_gather.3 = f32[4,32768]{0,1:T(8,128)} all-gather(f32[4,256]{0,1:T(8,128)} %reduce-scatter.2.cloned.1.call-done), channel_id=1, replica_groups=mesh['layer'=4,'seq'=16,'tile'=8] {'seq','tile'}, dimensions={1}, use_global_device_ids=true | all-gather | bytes 528384 | tf_op jit(solution)/shard_map/all_gather | solution.py:42
  469.0 6.8 %gather_fusion = f32[512,4]{1,0:T(8,128)S(1)} fusion(f32[4,32768]{0,1:T(8,128)} %all_gather.3, s32[1024]{0:T(1024)S(1)} %pad_clamp_fusion), kind=kCustom, calls=%fused_computation | custom fusion | bytes 18432 | tf_op jit(solution)/shard_map/jit(_take)/gather | solution.py:46
  475.8 0.2 select_bitcast_fusion
  476.0 0.0 copy-done.2
  476.0 1.1 fusion
  (4 shorter events, 0.0 us)
Async XLA Ops:
  6.5 1.8 copy-start
  6.5 3.9 copy-start.1
  6.5 88.8 %all-reduce.2.cloned.1.call-start = ((), (), s32[]{:S(2)}) async-start(), calls=%async_computation.1 | async-start | bytes 2359296 | tf_op jit(solution)/shard_map/psum | solution.py:23
  8.3 2.1 copy-start.3
  11.9 0.7 copy-start.5
  12.0 315.8 %reduce-scatter.2.cloned.1.call-start = ((), (), s32[]{:S(2)}) async-start(), calls=%async_computation.2 | async-start | bytes 16908288 | tf_op jit(solution)/shard_map/reduce_scatter | solution.py:39
  106.1 0.7 copy-start.4
  107.1 368.9 %copy-start.2 = (f32[1,256,256]{2,1,0:T(8,128)S(1)}, f32[1,256,256]{2,1,0:T(8,128)}, u32[]{:S(2)}) copy-start(f32[1,256,256]{2,1,0:T(8,128)} %param.13) | copy-start | bytes 786436
Sparse Core Ops, SparseCore 0:
  12.1 83.2 all-reduce.1
  106.2 221.4 reduce-scatter.1
where the time goes:
time: 484 us
  waiting for transfers between devices  303 us (63%)
  blocking collectives  141 us (29%)
  local copies, waits for them, and re-layouts  18.5 us (4%)
  between operations  13.5 us (3%)
  matrix products  5.57 us (1%)
    reduce_scatter x1, waiting for transfers between devices, body(): lax.psum_scatter(partial_value, ('seq', 'tile'), scatter_dimension=1, til...  221 us
    all_gather x1, blocking collectives, body(): shard_piece = lax.all_gather(features, ('seq', 'tile'), axis=1, tiled=True)  141 us
    psum x1, waiting for transfers between devices, body(): totals = lax.psum(whole_term, 'tile')  82.7 us
  transfers between devices with their start and end apart: 2, of which 2 were waited for; matrix products, arithmetic and copies ran while one was open for 0% of the time, Pallas kernels for 0%

commit v1 on v0

--- a/solution.py
+++ b/solution.py
@@ -39,7 +39,12 @@
     features = lax.psum_scatter(partial_value, ("seq", "tile"), scatter_dimension=1, tiled=True)
     owner_index = lax.axis_index(("seq", "tile"))
     own_pairs = lax.dynamic_slice_in_dim(tile_map, owner_index * tiles_here, tiles_here, 0)
-    shard_piece = lax.all_gather(features, ("seq", "tile"), axis=1, tiled=True)
+    shard_piece = jnp.concatenate(
+        lax.all_to_all(
+            jnp.stack([features] * lax.axis_size(("seq", "tile"))), ("seq", "tile"), 0, 0
+        ),
+        axis=1,
+    )
     piece_width = shard_piece.shape[1]
     columns = own_pairs[:, :, None] * block_size + offsets
     inside = (columns >= 0) & (columns < piece_width)

time: 484 us -> 390 us (0.81)
  the two profiles are of different devices: /device:TPU:25 before, /device:TPU:1 now
where the time goes in v1:
time: 390 us; the launch traced here: 389 us
  waiting for transfers between devices  325 us (83%)
  local copies, waits for them, and re-layouts  28.2 us (7%)
  starting transfers between devices  15 us (4%)
  between operations  13.5 us (3%)
  matrix products  5.57 us (1%)
    unnamed x3, waiting for transfers between devices  221 us
    psum x1, waiting for transfers between devices, body(): totals = lax.psum(whole_term, 'tile')  83.8 us
    all_to_all x1, waiting for transfers between devices, body(): lax.all_to_all(jnp.stack([features] * lax.axis_size(('seq', 'tile'))), ('...  20.5 us
    all_to_all x1, starting transfers between devices, body(): lax.all_to_all(jnp.stack([features] * lax.axis_size(('seq', 'tile'))), ('...  14.9 us
    unnamed x15, local copies, waits for them, and re-layouts  12 us
    reshape x1, local copies, waits for them, and re-layouts, body(): jnp.concatenate(lax.all_to_all(jnp.stack([features] * lax.axis_size(('seq...  8.5 us
  transfers between devices with their start and end apart: 3, of which 3 were waited for; matrix products, arithmetic and copies ran while one was open for 0% of the time, Pallas kernels for 0%

profile of v1, /device:TPU:1, one launch (start us, length us, event | category | flops | bytes accessed | tf_op | source)
XLA Modules:
  0.0 389.4 jit_solution(7591533849412024342)
XLA Ops:
  6.5 0.0 copy-start
  6.5 0.0 copy-start.1
  6.5 0.0 all-reduce.2.cloned.1.call-start
  6.5 1.8 copy-done
  8.3 0.0 copy-start.3
  8.3 2.1 convolution_bitcast_fusion
  10.4 0.0 copy-done.1
  10.4 0.0 copy-done.3
  10.4 0.4 convolution_bitcast_fusion.1
  10.8 1.1 pad_maximum_fusion
  11.9 0.0 copy-start.5
  11.9 0.0 all-reduce.2.cloned.1.call-update
  11.9 0.0 reduce-scatter.4.cloned.1.call-start
  12.0 0.6 copy-done.5
  12.6 0.1 compare_select_fusion.2
  12.6 83.8 %all-reduce.2.cloned.1.call-done = f32[192,4,384]{2,0,1:T(8,128)} async-done(((f32[192,4,384]{2,0,1:T(8,128)}), f32[192,4,384]{2,0,1:T(8,128)}) %all-reduce.2.cloned.1.call-update) | async-done | bytes 1179664 | tf_op jit(solution)/shard_map/psum | solution.py:23
  96.4 2.0 fusion.3
  98.5 8.7 %copy.13 = f32[4,256,128]{0,2,1:T(8,128)} copy(f32[4,256,128]{2,1,0:T(8,128)S(1)} %fusion.3) | data formatting | bytes 1048576
  107.2 0.0 reduce-scatter.4.cloned.1.call-update
  107.2 0.0 copy-start.4
  107.2 221.1 %reduce-scatter.4.cloned.1.call-done = f32[256,4]{1,0:T(8,128)} async-done(((f32[32768,4]{1,0:T(8,128)}), f32[256,4]{1,0:T(8,128)}) %reduce-scatter.4.cloned.1.call-update) | async-done | bytes 4112
  328.3 1.0 copy.12
  329.3 0.9 stack.2
  330.1 14.9 %all-to-all-start = ((f32[128,4,256]{2,1,0:T(4,128)}), f32[128,4,256]{2,1,0:T(4,128)S(1)}, u32[]{:S(2)}, u32[]{:S(2)}) async-start(f32[128,4,256]{2,1,0:T(4,128)} %stack.2), calls=%async_computation | async-start | bytes 1048576 | tf_op jit(solution)/shard_map/all_to_all | solution.py:43
  345.1 0.0 copy-done.4
  345.1 0.2 multiply_reduce_fusion
  345.3 0.1 fusion.6
  345.4 0.1 compare_and_fusion.1
  345.5 20.5 %all-to-all-done = f32[128,4,256]{2,1,0:T(4,128)S(1)} async-done(((f32[128,4,256]{2,1,0:T(4,128)}), f32[128,4,256]{2,1,0:T(4,128)S(1)}, u32[]{:S(2)}, u32[]{:S(2)}) %all-to-all-start) | async-done | bytes 524320 | tf_op jit(solution)/shard_map/all_to_all | solution.py:43
  366.0 0.0 copy-start.2
  366.0 8.5 %copy.10 = f32[4,128,256]{0,2,1:T(8,128)} copy(f32[4,128,256]{2,0,1:T(4,128)S(1)} %bitcast.41) | data formatting | bytes 1048576 | tf_op jit(solution)/shard_map/reshape | solution.py:42
  374.5 6.8 %gather_fusion = f32[512,4]{1,0:T(8,128)S(1)} fusion(f32[4,32768]{0,1:T(8,128)} %bitcast.40, s32[1024]{0:T(1024)S(1)} %pad_clamp_fusion), kind=kCustom, calls=%fused_computation | custom fusion | bytes 18432 | tf_op jit(solution)/shard_map/jit(_take)/gather | solution.py:51
  381.3 0.2 select_bitcast_fusion
  381.5 0.0 copy-done.2
  381.5 1.1 fusion
  (4 shorter events, 0.0 us)
Async XLA Ops:
  6.5 1.8 copy-start
  6.5 3.9 copy-start.1
  6.5 89.9 %all-reduce.2.cloned.1.call-start = ((), (), s32[]{:S(2)}) async-start(), calls=%async_computation.2 | async-start | bytes 2359296 | tf_op jit(solution)/shard_map/psum | solution.py:23
  8.3 2.1 copy-start.3
  11.9 0.7 copy-start.5
  11.9 316.3 %reduce-scatter.4.cloned.1.call-start = ((), (), s32[]{:S(2)}) async-start(), calls=%async_computation.3 | async-start | bytes 16908288
  107.2 237.9 %copy-start.4 = (s32[128,2]{0,1:T(2,128)S(1)}, s32[128,2]{0,1:T(2,128)}, u32[]{:S(2)}) copy-start(s32[128,2]{0,1:T(2,128)} %param.12) | copy-start | bytes 3076
  330.1 35.8 %all-to-all-start = ((f32[128,4,256]{2,1,0:T(4,128)}), f32[128,4,256]{2,1,0:T(4,128)S(1)}, u32[]{:S(2)}, u32[]{:S(2)}) async-start(f32[128,4,256]{2,1,0:T(4,128)} %stack.2), calls=%async_computation | async-start | bytes 1048576 | tf_op jit(solution)/shard_map/all_to_all | solution.py:43
  366.0 15.5 %copy-start.2 = (f32[1,256,256]{2,1,0:T(8,128)S(1)}, f32[1,256,256]{2,1,0:T(8,128)}, u32[]{:S(2)}) copy-start(f32[1,256,256]{2,1,0:T(8,128)} %param.13) | copy-start | bytes 786436
Sparse Core Ops, SparseCore 0:
  12.1 84.3 all-reduce.1
  107.3 220.9 reduce-scatter.3
